TPU v7x, 512 devices: a whole 4x4x16 slice. The times are simulated.
512 devices in a mesh: dom: 64 (over z, x_hi, core), mode: 8 (over x_lo, y).
Axes of the slice: x: 4 (x_hi: 2, x_lo: 2; x = x_hi * 2 + x_lo), y: 4, z: 16, core: 2. Of those that a mesh axis runs over, the one named last changes fastest.
Arguments:
- velocity: bfloat16 [3, 256, 17, 256], P(None, 'dom'), may hold values from -6 to 6
- stress: bfloat16 [16, 6, 256, 17, 256], P('mode', None, 'dom'), may hold values from -6 to 6
- relax_time: float32 [16], replicated, may hold values from 0.2 to 2
- viscosity: float32 [16], replicated, may hold values from 0.5 to 4
- extensibility: float32 [16], replicated, may hold values from 0.05 to 0.5
Outputs:
- stress_residual: bfloat16 [16, 6, 256, 17, 256], P('mode', None, 'dom')
- stress_divergence: float32 [3, 256, 17, 256], P(None, 'dom')
All inputs are finite; a program needn't handle non-finite values.
Results may differ from a plain program's by a relative error of at most 0.0074.
Values may be sent and summed in bfloat16 or wider, within the bound.
A program may use at most 128 MiB of HBM per device.

v0:
```python
import functools

import jax
import jax.numpy as jnp
import ml_dtypes
import numpy as np
from jax import lax
from jax.experimental import pallas as pl
from jax.experimental.pallas import tpu as pltpu
from jax.sharding import PartitionSpec as P

F32 = jnp.float32
BF16 = jnp.bfloat16
MESH = pl.DeviceIdType.MESH
SLOT = ((0, 3, 4), (3, 1, 5), (4, 5, 2))
NODES = 17
ROWS = 24
WINDOW = 256
POINTS = 224
LANES = 128


def gauss_tables():
    s = np.array([0.5 - 0.5 * np.sqrt(0.6), 0.5, 0.5 + 0.5 * np.sqrt(0.6)])
    weight = np.array([5.0, 8.0, 5.0]) / 18.0
    value = np.stack([2.0 * s * s - 3.0 * s + 1.0, 4.0 * s * (1.0 - s), 2.0 * s * s - s], axis=1)
    slope = np.stack([4.0 * s - 3.0, 4.0 - 8.0 * s, 4.0 * s - 1.0], axis=1)

    def product(first, second, third):
        joined = (
            first[:, None, None, :, None, None]
            * second[None, :, None, None, :, None]
            * third[None, None, :, None, None, :]
        )
        return joined.reshape(27, 27)

    forward = np.concatenate(
        [
            product(value, value, value),
            product(slope, value, value),
            product(value, slope, value),
            product(value, value, slope),
        ],
        axis=0,
    )
    volume = (weight[:, None, None] * weight[None, :, None] * weight[None, None, :]).reshape(27)
    testing = (forward * np.tile(volume, 4)[:, None]).T
    return forward.astype(ml_dtypes.bfloat16), testing.astype(ml_dtypes.bfloat16)


def column_tables():
    forward, testing = (np.asarray(t, np.float32) for t in gauss_tables())
    ahead = np.zeros((4, POINTS, WINDOW), np.float32)
    back = np.zeros((WINDOW, 4, 256), np.float32)
    for f in range((NODES - 1) // 2):
        for n in range(27):
            a, b, c = n // 9, (n // 3) % 3, n % 3
            node = 3 * ROWS * a + ROWS * c + 2 * f + b
            for d in range(4):
                rows = slice(27 * d, 27 * d + 27)
                ahead[d, 27 * f : 27 * f + 27, node] = forward[rows, n]
                back[node, d, 27 * f : 27 * f + 27] = testing[n, rows]
    back = back[: 9 * ROWS].reshape(9 * ROWS, 4 * 256)
    return ahead.astype(ml_dtypes.bfloat16), back.astype(ml_dtypes.bfloat16)


def order_tables():
    split = np.zeros((2 * LANES, 3 * LANES), np.float32)
    for g in range(LANES):
        split[2 * g, g] = 1.0
        split[2 * g + 1, LANES + g] = 1.0
        split[(2 * g + 2) % (2 * LANES), 2 * LANES + g] = 1.0
    merge = split[:, : 2 * LANES].T.copy()
    return split.astype(ml_dtypes.bfloat16), merge.astype(ml_dtypes.bfloat16)


def inverse_mass():
    r = np.arange(ROWS)
    mr = np.where(r % 2 == 1, 2.0 / 3.0, np.where((r == 0) | (r == NODES - 1), 1.0 / 6.0, 1.0 / 3.0))
    both = np.stack([3.0 / mr, 1.5 / mr])
    return np.ascontiguousarray(np.broadcast_to(both[:, :, None], (2, ROWS, LANES))).astype(np.float32)


def dot(x, y):
    return jnp.dot(x, y, preferred_element_type=F32)


def padded(x):
    return jnp.concatenate([x.astype(F32), jnp.zeros((ROWS - NODES, x.shape[1]), F32)], axis=0)


def stacked(parts, height):
    rows = sum(p.shape[0] for p in parts)
    if rows < height:
        parts = parts + [jnp.zeros((height - rows, parts[0].shape[1]), F32)]
    return jnp.concatenate(parts, axis=0).astype(BF16)


def block(column, a, c):
    start = 3 * ROWS * a + ROWS * c
    return column[start : start + ROWS]


def around(column, a):
    even = block(column, a, 0) + pltpu.roll(block(column, a, 2), 1, axis=1)
    return even, block(column, a, 1)


def kernel(
    doms,
    modes,
    velocity,
    stress,
    relax,
    viscosity,
    extension,
    ahead,
    back,
    split,
    merge,
    inv_mass,
    out_stress,
    out_div,
    vel_up,
    vel_dn,
    str_up,
    s_nodes,
    v_nodes,
    p_nodes,
    t_points,
    flux,
    dflux,
    derivs,
    grads,
    flow,
    winds,
    g_points,
    sums,
    devss,
    shares,
    rs_send,
    rs_recv,
    ag_buf,
    cup_send,
    cup_recv,
    top_send,
    top_recv,
    rows_s,
    halo_send,
    halo_recv,
    rs_ssem,
    rs_rsem,
    ag_ssem,
    ag_rsem,
    top_ssem,
    top_rsem,
):
    dom = lax.axis_index("dom")
    mode = lax.axis_index("mode")
    has_below = dom > 0
    has_above = dom < doms - 1
    below = (jnp.maximum(dom - 1, 0), mode)
    above = (jnp.minimum(dom + 1, doms - 1), mode)

    barrier = pltpu.get_barrier_semaphore()
    for off in range(1, modes):
        peer = lax.rem(mode + off, modes)
        pl.semaphore_signal(barrier, inc=1, device_id=(dom, peer), device_id_type=MESH)

    @pl.when(has_below)
    def _():
        pl.semaphore_signal(barrier, inc=1, device_id=below, device_id_type=MESH)

    @pl.when(has_above)
    def _():
        pl.semaphore_signal(barrier, inc=1, device_id=above, device_id_type=MESH)

    def remote(src, dst, send, recv, target):
        return pltpu.make_async_remote_copy(
            src_ref=src,
            dst_ref=dst,
            send_sem=send,
            recv_sem=recv,
            device_id=target,
            device_id_type=MESH,
        )

    down_stress = remote(stress.at[:, :, 0], str_up, halo_send.at[0], halo_recv.at[0], below)
    down_velocity = remote(velocity.at[:, 0:3], vel_up, halo_send.at[1], halo_recv.at[1], below)
    up_velocity = remote(velocity.at[:, 2:4], vel_dn, halo_send.at[2], halo_recv.at[2], above)
    up_share = remote(cup_send, cup_recv, halo_send.at[3], halo_recv.at[3], above)

    @pl.when(jnp.logical_not(has_above))
    def _():
        vel_up[...] = jnp.zeros_like(vel_up)
        str_up[...] = jnp.zeros_like(str_up)

    @pl.when(jnp.logical_not(has_below))
    def _():
        vel_dn[...] = jnp.zeros_like(vel_dn)
        cup_recv[...] = jnp.zeros_like(cup_recv)
        top_recv[...] = jnp.zeros_like(top_recv)

    others = modes - 1 + has_below.astype(jnp.int32) + has_above.astype(jnp.int32)
    pl.semaphore_wait(barrier, others)

    @pl.when(has_below)
    def _():
        down_velocity.start()
        down_stress.start()

    @pl.when(has_above)
    def _():
        up_velocity.start()

    def laid_out(planes):
        rows = len(planes) * ROWS
        height = -(-rows // 16) * 16
        spread = dot(stacked([padded(p) for p in planes], height), split[...])
        result = []
        for k in range(len(planes)):
            here = spread[k * ROWS : (k + 1) * ROWS]
            result.append([here[:, LANES * c : LANES * (c + 1)] for c in range(3)])
        return result

    PAIR = 6 * ROWS

    def lay_stress(k, _):
        planes = laid_out([stress[k // 2, 3 * (k % 2) + c, p] for c in range(3) for p in range(4)])
        for c in range(3):
            for pair in range(2):
                two = planes[4 * c + 2 * pair] + planes[4 * c + 2 * pair + 1]
                s_nodes[3 * k + c, (pair + 1) * PAIR : (pair + 2) * PAIR] = stacked(two, PAIR)
            s_nodes[3 * k + c, 0:PAIR] = jnp.zeros((PAIR, LANES), BF16)
            s_nodes[3 * k + c, 3 * PAIR :] = jnp.zeros((WINDOW - PAIR, LANES), BF16)
        return 0

    lax.fori_loop(0, 4, lay_stress, 0)
    for d in range(4):
        flux[256 * d + POINTS : 256 * (d + 1)] = jnp.zeros((256 - POINTS, 6 * LANES), BF16)
    for d in range(3):
        dflux[256 * d + POINTS : 256 * (d + 1)] = jnp.zeros((256 - POINTS, 3 * LANES), BF16)

    def stress_window(m, layer):
        start = (layer + 1) * PAIR
        return jnp.concatenate(
            [s_nodes[6 * m + c, start : start + WINDOW] for c in range(6)], axis=1
        )

    def column(c):
        return slice(LANES * c, LANES * (c + 1))

    def divergence_of(layer):
        for m in range(2):
            t_points[m] = dot(ahead[0], stress_window(m, layer))
        for c in range(6):
            both = (t_points[0, :, column(c)] + t_points[1, :, column(c)]).astype(BF16)
            for j in range(3):
                for i in range(3):
                    if SLOT[i][j] == c:
                        dflux[256 * j : 256 * j + POINTS, column(i)] = both
        return dot(back[:, 256:], dflux[...])

    upper = divergence_of(1)
    for i in range(3):
        even, odd = around(upper[:, column(i)], 2)
        cup_send[i] = stacked([even, odd], 2 * ROWS)

    @pl.when(has_above)
    def _():
        up_share.start()

    under = divergence_of(-1)
    inside = jnp.where(has_below, 1.0, 0.0).astype(F32)
    for i in range(3):
        even, odd = around(under[:, column(i)], 2)
        shares[0, i] = even * inside
        shares[1, i] = odd * inside
    middle = divergence_of(0)
    for i in range(3):
        for a in range(3):
            even, odd = around(middle[:, column(i)], a)
            if a == 0:
                even, odd = even + shares[0, i], odd + shares[1, i]
            shares[2 * a, i] = even
            shares[2 * a + 1, i] = odd

    for i in range(3):
        planes = laid_out([velocity[i, p] for p in range(4)])
        for pair in range(2):
            two = planes[2 * pair] + planes[2 * pair + 1]
            v_nodes[i, (pair + 1) * PAIR : (pair + 2) * PAIR] = stacked(two, PAIR)

    for layer in range(2):
        start = (layer + 1) * PAIR
        if layer == 1:

            @pl.when(has_above)
            def _():
                down_velocity.wait_recv()

            @pl.when(has_below)
            def _():
                up_velocity.wait_recv()

            for i in range(3):
                planes = laid_out([vel_dn[i, 0], vel_dn[i, 1]] + [vel_up[i, p] for p in range(3)])
                v_nodes[i, 0:PAIR] = stacked(planes[0] + planes[1], PAIR)
                v_nodes[i, 3 * PAIR : 4 * PAIR] = stacked(planes[2] + planes[3], PAIR)
                v_nodes[i, 4 * PAIR :] = stacked(planes[4], WINDOW - PAIR)
        nodes = jnp.concatenate([v_nodes[i, start : start + WINDOW] for i in range(3)], axis=1)
        at = dot(ahead[0], nodes).astype(BF16).astype(F32)
        u = [at[:, column(i)] for i in range(3)]
        upwind = 0.5 / (1.0 + jnp.sqrt(u[0] * u[0] + u[1] * u[1] + u[2] * u[2]))
        for i in range(3):
            flow[layer, i] = u[i]
            winds[layer, i] = (upwind * u[i]).astype(BF16)

    def gradient_layer(layer, _):
        start = pl.multiple_of(layer * PAIR, 16)
        nodes = jnp.concatenate([v_nodes[i, pl.ds(start, WINDOW)] for i in range(3)], axis=1)
        for j in range(3):
            at = dot(ahead[1 + j], nodes)
            derivs[layer, j] = stacked([at], 256)
            grads[layer, j] = dot(back[:, 0:256], derivs[layer, j])
        return 0

    lax.fori_loop(0, 4, gradient_layer, 0)

    first_mass = jnp.where(has_below, 3.0, 6.0).astype(F32)
    last_mass = jnp.where(has_above, 3.0, 0.0).astype(F32)
    plane_mass = [first_mass, 1.5, 3.0, 1.5, last_mass]
    sources = [[(0, 2), (1, 0)], [(1, 1)], [(1, 2), (2, 0)], [(2, 1)], [(2, 2), (3, 0)]]

    def project(j, _):
        for i in range(3):
            blocks = []
            for p in range(5):
                total = [0.0, 0.0, 0.0]
                for layer, a in sources[p]:
                    for c in range(3):
                        start = 3 * ROWS * a + ROWS * c
                        part = grads[layer, j, start : start + ROWS, column(i)]
                        if layer == 0:
                            part = part * inside
                        total[c] = total[c] + part
                even = total[0] + pltpu.roll(total[2], 1, axis=1)
                even = even * (inv_mass[0] * plane_mass[p])
                odd = total[1] * (inv_mass[1] * plane_mass[p])
                blocks.append([even, odd, pltpu.roll(even, LANES - 1, axis=1)])
            p_nodes[3 * i + j, 0:PAIR] = stacked(blocks[0] + blocks[1], PAIR)
            p_nodes[3 * i + j, PAIR : 2 * PAIR] = stacked(blocks[2] + blocks[3], PAIR)
            p_nodes[3 * i + j, 2 * PAIR :] = stacked(blocks[4], WINDOW - PAIR)
        return 0

    lax.fori_loop(0, 3, project, 0)

    for layer in range(2):
        for i in range(3):
            nodes = jnp.concatenate(
                [p_nodes[3 * i + j, layer * PAIR : layer * PAIR + WINDOW] for j in range(3)], axis=1
            )
            here = dot(ahead[0], nodes)
            for j in range(3):
                g_points[layer, 3 * i + j] = here[:, column(j)]

    @pl.when(has_above)
    def _():
        down_stress.wait_recv()

    for k in range(4):
        planes = laid_out([str_up[k // 2, 3 * (k % 2) + c] for c in range(3)])
        for c in range(3):
            s_nodes[3 * k + c, 3 * PAIR :] = stacked(planes[c], WINDOW - PAIR)

    upper = divergence_of(1)

    @pl.when(has_below)
    def _():
        up_share.wait_recv()

    for i in range(3):
        from_below = cup_recv[i].astype(F32)
        shares[0, i] = shares[0, i] + from_below[0:ROWS]
        shares[1, i] = shares[1, i] + from_below[ROWS:]
        for a in range(2):
            even, odd = around(upper[:, column(i)], a)
            if a == 0:
                even, odd = even + shares[4, i], odd + shares[5, i]
            shares[4 + 2 * a, i] = even
            shares[5 + 2 * a, i] = odd
    for k in range(8):
        rs_send[k] = stacked([shares[k, i] for i in range(3)], 80)

    def share_copy(off):
        peer = lax.rem(mode + off, modes)
        return remote(
            rs_send.at[peer], rs_recv.at[off], rs_ssem.at[off], rs_rsem.at[off], (dom, peer)
        )

    for off in range(1, modes):
        share_copy(off).start()

    def residual_of(layer, m):
        lam = jnp.full((16, LANES), relax[2 * mode + m], F32)
        eta = jnp.full((16, LANES), viscosity[2 * mode + m], F32)
        eps = jnp.full((16, LANES), extension[2 * mode + m], F32)
        half = 0.5 / lam
        slope = 0.5 * eps / eta
        kappa = eta / lam
        nodes = stress_window(m, layer)
        for d in range(4):
            t_points[d] = dot(ahead[d], nodes)

        def chunk(start):
            rows = pl.ds(start, 16)
            t = [t_points[0, rows, column(c)] for c in range(6)]
            g = [[g_points[layer, 3 * i + j, rows] for j in range(3)] for i in range(3)]
            u = [flow[layer, i, rows] for i in range(3)]
            y = half + slope * (t[0] + t[1] + t[2])
            shift = (y * kappa) * 2.0
            tt = [t[0] + kappa, t[1] + kappa, t[2] + kappa] + t[3:]
            h = [g[k][k] - y for k in range(3)]

            def entry(i, j):
                return tt[SLOT[i][j]]

            result = []
            for c, (i, j) in enumerate(((0, 0), (1, 1), (2, 2), (0, 1), (0, 2), (1, 2))):
                value = u[0] * t_points[1, rows, column(c)]
                value = value + u[1] * t_points[2, rows, column(c)]
                value = value + u[2] * t_points[3, rows, column(c)]
                if i == j:
                    k, l = (i + 1) % 3, (i + 2) % 3
                    part = h[i] * entry(i, i) + g[i][k] * entry(k, i) + g[i][l] * entry(l, i)
                    value = value - (part + part) - shift
                else:
                    k = 3 - i - j
                    part = (h[i] + h[j]) * entry(i, j)
                    part = part + g[i][j] * entry(j, j) + g[i][k] * entry(k, j)
                    part = part + g[j][i] * entry(i, i) + g[j][k] * entry(k, i)
                    value = value - part
                result.append(value)
            for c in range(6):
                rounded = result[c].astype(BF16)
                flux[rows, column(c)] = rounded
                for j in range(3):
                    place = pl.ds(256 * (1 + j) + start, 16)
                    flux[place, column(c)] = rounded * winds[layer, j, rows]

        def two_chunks(k, _):
            start = pl.multiple_of(32 * k, 32)
            chunk(start)
            chunk(start + 16)
            return 0

        lax.fori_loop(0, POINTS // 32, two_chunks, 0)
        sums[2 * layer + m] = dot(back[...], flux[...])

    weight = viscosity[0]
    for k in range(1, 2 * modes):
        weight = weight + viscosity[k]
    weight = weight * (1.0 / (2 * modes))

    def devss_of(layer):
        for i in range(3):
            for j in range(i, 3):
                d_ij = derivs[layer + 1, j, 0:POINTS, column(i)].astype(F32)
                d_ji = derivs[layer + 1, i, 0:POINTS, column(j)].astype(F32)
                excess = d_ij + d_ji - g_points[layer, 3 * i + j] - g_points[layer, 3 * j + i]
                value = (weight * excess).astype(BF16)
                dflux[256 * j : 256 * j + POINTS, column(i)] = value
                if i != j:
                    dflux[256 * i : 256 * i + POINTS, column(j)] = value
        devss[layer] = dot(back[:, 256:], dflux[...])

    def top_copy(k, first, count):
        part = pl.ds(first, count)
        return remote(top_send.at[part], top_recv.at[part], top_ssem.at[k], top_rsem.at[k], above)

    tops = [top_copy(0, 0, 6), top_copy(1, 6, 6), top_copy(2, 12, 3)]

    def start_top(k):
        @pl.when(has_above)
        def _():
            tops[k].start()

    for m in range(2):
        residual_of(1, m)
        for c in range(6):
            even, odd = around(sums[2 + m, :, column(c)], 2)
            top_send[6 * m + c] = stacked([even, odd], 2 * ROWS)
        start_top(m)
    devss_of(1)
    for i in range(3):
        even, odd = around(devss[1, :, column(i)], 2)
        top_send[12 + i] = stacked([even, odd], 2 * ROWS)
    start_top(2)

    total = jnp.concatenate([shares[mode, i] for i in range(3)] + [jnp.zeros((8, LANES), F32)], axis=0)
    for off in range(1, modes):
        share_copy(off).wait_recv()
        total = total + rs_recv[off].astype(F32)
    ag_buf[mode] = total.astype(BF16)

    def whole_copy(off, slot):
        peer = lax.rem(mode + off, modes)
        return remote(
            ag_buf.at[slot], ag_buf.at[slot], ag_ssem.at[off], ag_rsem.at[off], (dom, peer)
        )

    for off in range(1, modes):
        whole_copy(off, mode).start()

    for m in range(2):
        residual_of(0, m)
    devss_of(0)

    for off in range(1, modes):
        whole_copy(off, lax.rem(mode + modes - off, modes)).wait_recv()

    @pl.when(has_below)
    def _():
        for k in range(3):
            tops[k].wait_recv()

    place = [[(0, 0)], [(0, 1)], [(0, 2), (1, 0)], [(1, 1)]]

    def finish(k, _):
        m, c0 = k // 2, 3 * (k % 2)
        lam = relax[2 * mode + m]
        pieces = []
        for c in range(3):
            for p in range(4):
                even, odd = 0.0, 0.0
                for layer, a in place[p]:
                    start = 3 * ROWS * a
                    cols = pl.ds(pl.multiple_of((c0 + c) * LANES, LANES), LANES)
                    first = sums[2 * layer + m, start : start + ROWS, cols]
                    second = sums[2 * layer + m, start + ROWS : start + 2 * ROWS, cols]
                    third = sums[2 * layer + m, start + 2 * ROWS : start + 3 * ROWS, cols]
                    even = even + (first + pltpu.roll(third, 1, axis=1))
                    odd = odd + second
                if p == 0:
                    from_below = top_recv[6 * m + c0 + c].astype(F32)
                    even = even + from_below[0:ROWS]
                    odd = odd + from_below[ROWS:]
                pieces.append(jnp.concatenate([even * lam, odd * lam], axis=1))
        merged = dot(stacked(pieces, 12 * ROWS), merge[...]).astype(BF16)
        rows_s[...] = merged.astype(F32)
        for c in range(3):
            for p in range(4):
                start = (4 * c + p) * ROWS
                out_stress[m, c0 + c, p] = rows_s[start : start + NODES].astype(BF16)
        return 0

    lax.fori_loop(0, 4, finish, 0)

    high, low = [], []
    for i in range(3):
        for p in range(4):
            even = ag_buf[2 * p].astype(F32)[ROWS * i : ROWS * (i + 1)]
            odd = ag_buf[2 * p + 1].astype(F32)[ROWS * i : ROWS * (i + 1)]
            for layer, a in place[p]:
                more_even, more_odd = around(devss[layer, :, column(i)], a)
                even, odd = even + more_even, odd + more_odd
            if p == 0:
                from_below = top_recv[12 + i].astype(F32)
                even = even + from_below[0:ROWS]
                odd = odd + from_below[ROWS:]
            both = jnp.concatenate([even, odd], axis=1)
            rounded = both.astype(BF16).astype(F32)
            high.append(rounded)
            low.append(both - rounded)
    rows_s[...] = dot(stacked(high, 12 * ROWS), merge[...]) + dot(
        stacked(low, 12 * ROWS), merge[...]
    )
    for i in range(3):
        for p in range(4):
            start = (4 * i + p) * ROWS
            out_div[i, p] = rows_s[start : start + NODES]

    @pl.when(has_below)
    def _():
        down_velocity.wait_send()
        down_stress.wait_send()

    @pl.when(has_above)
    def _():
        up_velocity.wait_send()
        up_share.wait_send()
        for k in range(3):
            tops[k].wait_send()

    for off in range(1, modes):
        share_copy(off).wait_send()
        whole_copy(off, mode).wait_send()


def on_device(doms, modes, velocity, stress, relax_time, viscosity, extensibility):
    ahead, back = column_tables()
    split, merge = order_tables()
    vmem = pl.BlockSpec(memory_space=pltpu.VMEM)
    smem = pl.BlockSpec(memory_space=pltpu.SMEM)
    dma = pltpu.SemaphoreType.DMA
    around_nodes = 2 * LANES
    scratch = [
        pltpu.VMEM((3, 3, NODES, around_nodes), BF16),
        pltpu.VMEM((3, 2, NODES, around_nodes), BF16),
        pltpu.VMEM((2, 6, NODES, around_nodes), BF16),
        pltpu.VMEM((12, 2 * 144 + WINDOW, LANES), BF16),
        pltpu.VMEM((3, 3 * 144 + WINDOW, LANES), BF16),
        pltpu.VMEM((9, 144 + WINDOW, LANES), BF16),
        pltpu.VMEM((4, POINTS, 6 * LANES), F32),
        pltpu.VMEM((4 * 256, 6 * LANES), BF16),
        pltpu.VMEM((3 * 256, 3 * LANES), BF16),
        pltpu.VMEM((4, 3, 256, 3 * LANES), BF16),
        pltpu.VMEM((4, 3, 9 * ROWS, 3 * LANES), F32),
        pltpu.VMEM((2, 3, POINTS, LANES), F32),
        pltpu.VMEM((2, 3, POINTS, LANES), BF16),
        pltpu.VMEM((2, 9, POINTS, LANES), F32),
        pltpu.VMEM((4, 9 * ROWS, 6 * LANES), F32),
        pltpu.VMEM((2, 9 * ROWS, 3 * LANES), F32),
        pltpu.VMEM((8, 3, ROWS, LANES), F32),
        pltpu.VMEM((8, 80, LANES), BF16),
        pltpu.VMEM((8, 80, LANES), BF16),
        pltpu.VMEM((8, 80, LANES), BF16),
        pltpu.VMEM((3, 2 * ROWS, LANES), BF16),
        pltpu.VMEM((3, 2 * ROWS, LANES), BF16),
        pltpu.VMEM((15, 2 * ROWS, LANES), BF16),
        pltpu.VMEM((15, 2 * ROWS, LANES), BF16),
        pltpu.VMEM((12 * ROWS, around_nodes), F32),
        dma((4,)),
        dma((4,)),
        dma((modes,)),
        dma((modes,)),
        dma((modes,)),
        dma((modes,)),
        dma((3,)),
        dma((3,)),
    ]
    return pl.pallas_call(
        functools.partial(kernel, doms, modes),
        out_shape=(
            jax.ShapeDtypeStruct(stress.shape, BF16),
            jax.ShapeDtypeStruct(velocity.shape, F32),
        ),
        in_specs=[vmem, vmem, smem, smem, smem, vmem, vmem, vmem, vmem, vmem],
        out_specs=(vmem, vmem),
        scratch_shapes=scratch,
        compiler_params=pltpu.CompilerParams(
            collective_id=0, has_side_effects=True, vmem_limit_bytes=48 * 1024 * 1024
        ),
        name="ptt",
    )(
        velocity,
        stress,
        relax_time,
        viscosity,
        extensibility,
        jnp.asarray(ahead),
        jnp.asarray(back),
        jnp.asarray(split),
        jnp.asarray(merge),
        jnp.asarray(inverse_mass()),
    )


def solution(mesh):
    return jax.shard_map(
        functools.partial(on_device, mesh.shape["dom"], mesh.shape["mode"]),
        mesh=mesh,
        in_specs=(P(None, "dom", None, None), P("mode", None, "dom", None, None), P(), P(), P()),
        out_specs=(P("mode", None, "dom", None, None), P(None, "dom", None, None)),
        check_vma=False,
    )
```

profile of v0, /device:TPU:384, one launch (start us, length us, event | category | flops | bytes accessed | tf_op | source)
XLA Modules:
  0.0 33.6 jit_solution(769121591075223536)
XLA Ops:
  0.6 0.0 copy-start.2
  0.6 0.0 copy-start.3
  0.7 1.0 %copy.12.velocity = bf16[3,4,17,256]{3,2,1,0:T(8,128)(2,1)S(1)} copy(bf16[3,4,17,256]{3,1,2,0:T(4,128)(2,1)} %param.10) | data formatting | bytes 208896 | tf_op args[0]
  1.6 0.0 copy-start
  1.6 0.0 copy-start.1
  1.6 0.0 copy-start.4
  1.7 0.0 copy-start.5
  1.7 0.0 copy-start.6
  1.7 0.0 copy-start.7
  1.7 1.2 %copy.13.stress = bf16[2,6,4,17,256]{4,3,2,1,0:T(8,128)(2,1)S(1)} copy(bf16[2,6,4,17,256]{4,2,3,1,0:T(4,128)(2,1)} %param.11) | data formatting | bytes 835584 | tf_op args[1]
  2.9 0.0 copy-done.2
  2.9 0.0 copy-done.3
  2.9 0.0 copy-done
  2.9 0.0 copy-done.1
  2.9 0.0 copy-done.4
  2.9 0.0 copy-done.5
  2.9 0.0 copy-done.6
  2.9 0.0 copy-done.7
  2.9 29.0 %ptt.1 = (bf16[2,6,4,17,256]{4,3,2,1,0:T(8,128)(2,1)S(1)}, f32[3,4,17,256]{3,2,1,0:T(8,128)S(1)}) custom-call(bf16[3,4,17,256]{3,2,1,0:T(8,128)(2,1)S(1)} %copy.12.velocity, bf16[2,6,4,17,256]{4,3,2,1,0:T(8,128)(2,1)S(1)} %copy.13.stress, f32[16]{0:T(128)S(1)} %copy-done.5, f32[16]{0:T(128)S(1)} %copy-done.6, f32[16]{0:T(128)S(1)} %copy-done.7, ...), custom_call_target="tpu_custom_call" | custom-call | tf_op jit(solution)/shard_map/ptt/pallas_call | solution.py:642
  31.9 0.9 %copy.14 = bf16[2,6,4,17,256]{4,2,3,1,0:T(4,128)(2,1)} copy(bf16[2,6,4,17,256]{4,3,2,1,0:T(8,128)(2,1)S(1)} %get-tuple-element.2) | data formatting | bytes 835584 | tf_op jit(solution)/shard_map/ptt/pallas_call | solution.py:642
  32.9 0.8 %copy.15 = f32[3,4,17,256]{3,1,2,0:T(4,128)} copy(f32[3,4,17,256]{3,2,1,0:T(8,128)S(1)} %get-tuple-element.3) | data formatting | bytes 417792 | tf_op jit(solution)/shard_map/ptt/pallas_call | solution.py:642
Async XLA Ops:
  0.6 2.2 %copy-start.2 = (bf16[256,384]{1,0:T(8,128)(2,1)S(1)}, bf16[256,384]{1,0:T(8,128)(2,1)}, u32[]{:S(2)}) copy-start(bf16[256,384]{1,0:T(8,128)(2,1)} %constant.12.clone.split) | copy-start | bytes 589828
  0.6 2.2 %copy-start.3 = (bf16[256,256]{1,0:T(8,128)(2,1)S(1)}, bf16[256,256]{1,0:T(8,128)(2,1)}, u32[]{:S(2)}) copy-start(bf16[256,256]{1,0:T(8,128)(2,1)} %constant.13.clone.merge) | copy-start | bytes 393220
  1.6 1.3 %copy-start = (bf16[4,224,256]{2,1,0:T(8,128)(2,1)S(1)}, bf16[4,224,256]{2,1,0:T(8,128)(2,1)}, u32[]{:S(2)}) copy-start(bf16[4,224,256]{2,1,0:T(8,128)(2,1)} %constant.10.clone.ahead) | copy-start | bytes 1376260
  1.6 1.3 %copy-start.1 = (bf16[216,1024]{1,0:T(8,128)(2,1)S(1)}, bf16[216,1024]{1,0:T(8,128)(2,1)}, u32[]{:S(2)}) copy-start(bf16[216,1024]{1,0:T(8,128)(2,1)} %constant.11.clone.back) | copy-start | bytes 1327108
  1.6 1.3 %copy-start.4 = (f32[2,24,128]{2,1,0:T(8,128)S(1)}, f32[2,24,128]{2,1,0:T(8,128)}, u32[]{:S(2)}) copy-start(f32[2,24,128]{2,1,0:T(8,128)} %constant.14.clone.inv_mass) | copy-start | bytes 73732
  1.7 1.3 %copy-start.5 = (f32[16]{0:T(128)S(1)}, f32[16]{0:T(128)}, u32[]{:S(2)}) copy-start(f32[16]{0:T(128)} %relax.1) | copy-start | bytes 196
  1.7 1.3 %copy-start.6 = (f32[16]{0:T(128)S(1)}, f32[16]{0:T(128)}, u32[]{:S(2)}) copy-start(f32[16]{0:T(128)} %viscosity.1) | copy-start | bytes 196
  1.7 1.3 %copy-start.7 = (f32[16]{0:T(128)S(1)}, f32[16]{0:T(128)}, u32[]{:S(2)}) copy-start(f32[16]{0:T(128)} %extension.1) | copy-start | bytes 196
where the time goes:
time: 33.8 us; the launch traced here: 33.6 us
  Pallas kernels  29 us (86%)
  local copies, waits for them, and re-layouts  3.87 us (11%)
  between operations  0.77 us (2%)
    pallas_call x1, Pallas kernels, on_device(): pl.pallas_call(functools.partial(kernel, doms, modes), out_shape=(jax.Sha...  29 us
    unnamed x18, local copies, waits for them, and re-layouts  2.19 us
    pallas_call x2, local copies, waits for them, and re-layouts, on_device(): pl.pallas_call(functools.partial(kernel, doms, modes), out_shape=(jax.Sha...  1.68 us

commit v1 on v0

v1 whole, which is shorter than its diff:
```python
import functools

import jax
import jax.numpy as jnp
import ml_dtypes
import numpy as np
from jax import lax
from jax.experimental import pallas as pl
from jax.experimental.pallas import tpu as pltpu
from jax.sharding import PartitionSpec as P

F32 = jnp.float32
BF16 = jnp.bfloat16
MESH = pl.DeviceIdType.MESH
SLOT = ((0, 3, 4), (3, 1, 5), (4, 5, 2))
NODES = 17
OWN = 4
GROUP = 72
SENT = 80
COLUMN = 216
WINDOW = 256
POINTS = 224
LANES = 128


def gauss_tables():
    s = np.array([0.5 - 0.5 * np.sqrt(0.6), 0.5, 0.5 + 0.5 * np.sqrt(0.6)])
    weight = np.array([5.0, 8.0, 5.0]) / 18.0
    value = np.stack([2.0 * s * s - 3.0 * s + 1.0, 4.0 * s * (1.0 - s), 2.0 * s * s - s], axis=1)
    slope = np.stack([4.0 * s - 3.0, 4.0 - 8.0 * s, 4.0 * s - 1.0], axis=1)

    def product(first, second, third):
        joined = (
            first[:, None, None, :, None, None]
            * second[None, :, None, None, :, None]
            * third[None, None, :, None, None, :]
        )
        return joined.reshape(27, 27)

    forward = np.concatenate(
        [
            product(value, value, value),
            product(slope, value, value),
            product(value, slope, value),
            product(value, value, slope),
        ],
        axis=0,
    )
    volume = (weight[:, None, None] * weight[None, :, None] * weight[None, None, :]).reshape(27)
    testing = (forward * np.tile(volume, 4)[:, None]).T
    return forward.astype(ml_dtypes.bfloat16), testing.astype(ml_dtypes.bfloat16)


def column_tables():
    forward, testing = (np.asarray(t, np.float32) for t in gauss_tables())
    ahead = np.zeros((2, 4, POINTS, WINDOW), np.float32)
    back = np.zeros((2, COLUMN, 4 * 256), np.float32)
    for layer, slots in enumerate(((0, 1, 2), (2, 3, 0))):
        for f in range((NODES - 1) // 2):
            for n in range(27):
                a, b, c = n // 9, (n // 3) % 3, n % 3
                node = GROUP * c + OWN * (2 * f + b) + slots[a]
                for d in range(4):
                    rows = slice(27 * d, 27 * d + 27)
                    ahead[layer, d, 27 * f : 27 * f + 27, node] = forward[rows, n]
                    back[layer, node, 256 * d + 27 * f : 256 * d + 27 * f + 27] = testing[n, rows]
    first = np.arange(WINDOW) % OWN == 0
    parts = np.zeros((2, POINTS, WINDOW), np.float32)
    parts[0] = ahead[1, 0] * ~first
    parts[1] = ahead[1, 0] * first
    ahead = np.concatenate([ahead.reshape(8, POINTS, WINDOW), parts])
    return ahead.astype(ml_dtypes.bfloat16), back.astype(ml_dtypes.bfloat16)


def order_tables():
    split = np.zeros((2 * LANES, 3 * LANES), np.float32)
    for g in range(LANES):
        split[2 * g, g] = 1.0
        split[2 * g + 1, LANES + g] = 1.0
        split[(2 * g + 2) % (2 * LANES), 2 * LANES + g] = 1.0
    merge = split[:, : 2 * LANES].T.copy()
    return split.astype(ml_dtypes.bfloat16), merge.astype(ml_dtypes.bfloat16)


def inverse_mass():
    r = np.arange(GROUP) // OWN
    mz = np.where(np.arange(GROUP) % 2 == 1, 2.0 / 3.0, 1.0 / 3.0)
    mr = np.where(r % 2 == 1, 2.0 / 3.0, np.where((r == 0) | (r >= NODES - 1), 1.0 / 6.0, 1.0 / 3.0))
    both = np.stack([3.0 / (mz * mr), 1.5 / (mz * mr)])
    return np.ascontiguousarray(np.broadcast_to(both[:, :, None], (2, GROUP, LANES))).astype(np.float32)


def dot(x, y):
    return jnp.dot(x, y, preferred_element_type=F32)


def raised(x, height):
    return jnp.concatenate([x, jnp.zeros((height - x.shape[0], x.shape[1]), F32)], axis=0).astype(BF16)


def column(c):
    return slice(LANES * c, LANES * (c + 1))


def kernel(
    doms,
    modes,
    velocity_hbm,
    stress_hbm,
    relax,
    viscosity,
    extension,
    ahead_hbm,
    back_hbm,
    split_hbm,
    mass_hbm,
    pieces,
    velocity,
    stress,
    ahead,
    back,
    split,
    inv_mass,
    s_rows,
    str_down,
    vel_above,
    vel_below,
    str_above,
    cup_send,
    cup_recv,
    top_send,
    top_recv,
    s_nodes,
    v_nodes,
    p_nodes,
    t_points,
    flux,
    dflux,
    derivs,
    grads,
    flow,
    winds,
    g_points,
    sums,
    devss,
    shares,
    rs_send,
    rs_recv,
    ag_buf,
    local_sem,
    halo_send,
    halo_recv,
    rs_ssem,
    rs_rsem,
    ag_ssem,
    ag_rsem,
    top_ssem,
    top_rsem,
):
    dom = lax.axis_index("dom")
    mode = lax.axis_index("mode")
    has_below = dom > 0
    has_above = dom < doms - 1
    below = (jnp.maximum(dom - 1, 0), mode)
    above = (jnp.minimum(dom + 1, doms - 1), mode)
    inside = jnp.where(has_below, 1.0, 0.0).astype(F32)

    barrier = pltpu.get_barrier_semaphore()

    @pl.when(has_below)
    def _():
        pl.semaphore_signal(barrier, inc=1, device_id=below, device_id_type=MESH)

    @pl.when(has_above)
    def _():
        pl.semaphore_signal(barrier, inc=1, device_id=above, device_id_type=MESH)

    for off in range(1, modes):
        peer = lax.rem(mode + off, modes)
        pl.semaphore_signal(barrier, inc=1, device_id=(dom, peer), device_id_type=MESH)

    pairs = (
        (velocity_hbm, velocity),
        (stress_hbm, stress),
        (split_hbm, split),
        (ahead_hbm, ahead),
        (back_hbm, back),
        (mass_hbm, inv_mass),
    )
    loads = [pltpu.make_async_copy(a, b, local_sem.at[k]) for k, (a, b) in enumerate(pairs)]
    for load in loads:
        load.start()

    def remote(src, dst, send, recv, target):
        return pltpu.make_async_remote_copy(
            src_ref=src,
            dst_ref=dst,
            send_sem=send,
            recv_sem=recv,
            device_id=target,
            device_id_type=MESH,
        )

    down_velocity = remote(velocity_hbm, vel_above, halo_send.at[0], halo_recv.at[0], below)
    down_stress = remote(str_down, str_above, halo_send.at[1], halo_recv.at[1], below)
    up_velocity = remote(velocity_hbm, vel_below, halo_send.at[2], halo_recv.at[2], above)
    up_share = remote(cup_send, cup_recv, halo_send.at[3], halo_recv.at[3], above)

    @pl.when(jnp.logical_not(has_above))
    def _():
        vel_above[...] = jnp.zeros_like(vel_above)
        str_above[...] = jnp.zeros_like(str_above)

    @pl.when(jnp.logical_not(has_below))
    def _():
        vel_below[...] = jnp.zeros_like(vel_below)
        cup_recv[...] = jnp.zeros_like(cup_recv)
        top_recv[...] = jnp.zeros_like(top_recv)

    slot = lax.rem(lax.broadcasted_iota(jnp.int32, (GROUP, LANES), 0), OWN)
    slots = jnp.concatenate([slot, slot], axis=1)
    first = slot == 0
    firsts = slots == 0

    def shifted(block, rows):
        return block if rows == 0 else pltpu.roll(block, rows % GROUP, axis=0)

    def packed(blocks):
        result = blocks[0]
        for q in range(1, len(blocks)):
            result = jnp.where(slots == q, shifted(blocks[q], q), result)
        return result

    def rows_of(ref):
        return jnp.concatenate(
            [ref.astype(F32).reshape(OWN * NODES, 2 * LANES), jnp.zeros((GROUP - OWN * NODES, 2 * LANES), F32)],
            axis=0,
        )

    loads[1].wait()
    for g in range(3):
        blocks = []
        for q in range(4):
            k = 4 * g + q
            blocks.append(rows_of(stress[k // 6, k % 6]))
            s_rows[k] = raised(blocks[q], SENT)
        str_down[g] = raised(packed(blocks), SENT)

    def laid_out(rows):
        spread = dot(jnp.concatenate(rows, axis=0), split[...])
        return [
            [spread[SENT * k : SENT * k + GROUP, column(c)] for c in range(3)] for k in range(len(rows))
        ]

    def window(parts):
        return raised(jnp.concatenate(parts, axis=0), WINDOW)

    for d in range(4):
        flux[256 * d + POINTS : 256 * (d + 1)] = jnp.zeros((256 - POINTS, 6 * LANES), BF16)
        derivs[d, POINTS:] = jnp.zeros((256 - POINTS, 9 * LANES), BF16)
    for d in range(3):
        dflux[256 * d + POINTS : 256 * (d + 1)] = jnp.zeros((256 - POINTS, 3 * LANES), BF16)

    loads[2].wait()
    for k in range(4):
        own = laid_out([s_rows[3 * k + c] for c in range(3)])
        for c in range(3):
            s_nodes[0, 3 * k + c] = window(own[c])

    def side(ref, index, count):
        return jnp.concatenate([ref[index, c] for c in range(count)], axis=1)

    def stress_window(layer, m):
        return jnp.concatenate([s_nodes[layer, 6 * m + c] for c in range(6)], axis=1)

    def around(result, c):
        even = result[0:GROUP, column(c)] + pltpu.roll(result[2 * GROUP :, column(c)], 1, axis=1)
        return even, result[GROUP : 2 * GROUP, column(c)]

    def points_of(layer):
        for m in range(2):
            nodes = stress_window(layer, m)
            for d in range(4):
                t_points[layer, m, d] = dot(ahead[4 * layer + d], nodes)

    def into_dflux(values):
        for j in range(3):
            for i in range(3):
                dflux[256 * j : 256 * j + POINTS, column(i)] = values[SLOT[i][j]]

    loads[0].wait()
    own_velocity = laid_out([raised(rows_of(velocity[i]), SENT) for i in range(3)])
    for i in range(3):
        v_nodes[0, i] = window(own_velocity[i])

    others = modes - 1 + has_below.astype(jnp.int32) + has_above.astype(jnp.int32)
    pl.semaphore_wait(barrier, others)

    @pl.when(has_below)
    def _():
        down_velocity.start()
        down_stress.start()

    @pl.when(has_above)
    def _():
        up_velocity.start()

    loads[3].wait()
    loads[4].wait()
    both = jnp.concatenate([stress_window(0, 0), stress_window(0, 1)], axis=0)

    def outer_share(part):
        at = dot(jnp.concatenate([part, part], axis=1), both).astype(BF16)
        into_dflux([at[:, column(c)] for c in range(6)])
        return dot(back[1, :, 256:], dflux[...])

    outer = outer_share(ahead[8])
    cup_send[...] = raised(packed([jnp.concatenate(around(outer, i), axis=1) for i in range(3)]), SENT)

    @pl.when(has_above)
    def _():
        up_share.start()

    outer = outer_share(ahead[9])
    for i in range(3):
        even, odd = around(outer, i)
        zero = jnp.zeros_like(even)
        shares[GROUP * 2 * i : GROUP * (2 * i + 1)] = jnp.where(first, even * inside, zero)
        shares[GROUP * (2 * i + 1) : GROUP * (2 * i + 2)] = jnp.where(first, odd * inside, zero)

    def add_shares(result):
        for i in range(3):
            even, odd = around(result, i)
            shares[GROUP * 2 * i : GROUP * (2 * i + 1)] += even
            shares[GROUP * (2 * i + 1) : GROUP * (2 * i + 2)] += odd

    at = dot(jnp.concatenate([ahead[0], ahead[0]], axis=1), both).astype(BF16)
    into_dflux([at[:, column(c)] for c in range(6)])
    add_shares(dot(back[0, :, 256:], dflux[...]))

    def velocity_points(layer, at):
        at = at.astype(BF16).astype(F32)
        u = [at[:, column(i)] for i in range(3)]
        upwind = 0.5 / (1.0 + jnp.sqrt(u[0] * u[0] + u[1] * u[1] + u[2] * u[2]))
        for i in range(3):
            flow[layer, i] = u[i]
            winds[layer, i] = (upwind * u[i]).astype(BF16)

    def gradient_points(variant, layer):
        nodes = side(v_nodes, variant, 3)
        for j in range(3):
            at = dot(ahead[4 * layer + 1 + j], nodes)
            derivs[variant, 0:POINTS, 3 * LANES * j : 3 * LANES * (j + 1)] = at.astype(BF16)
        grads[variant] = dot(back[layer, :, 0:256], derivs[variant])

    velocity_points(0, dot(ahead[0], side(v_nodes, 0, 3)))
    gradient_points(0, 0)
    points_of(0)

    @pl.when(has_above)
    def _():
        down_velocity.wait_recv()

    @pl.when(has_below)
    def _():
        up_velocity.wait_recv()

    six = laid_out([raised(rows_of(ref[i]), SENT) for ref in (vel_above, vel_below) for i in range(3)])
    higher, lower = six[0:3], six[3:6]
    own = [
        [v_nodes[0, i, 0:224].astype(F32)[GROUP * c : GROUP * (c + 1)] for c in range(3)]
        for i in range(3)
    ]
    for i in range(3):
        v_nodes[1, i] = window([jnp.where(first, higher[i][c], own[i][c]) for c in range(3)])
        v_nodes[2, i] = window([jnp.where(first, own[i][c], lower[i][c]) for c in range(3)])
        v_nodes[3, i] = window(higher[i])
    gradient_points(1, 1)
    gradient_points(2, 1)
    gradient_points(3, 0)

    @pl.when(has_above)
    def _():
        down_stress.wait_recv()

    higher = laid_out([str_above[g] for g in range(3)])
    for k in range(12):
        mine = s_nodes[0, k].astype(F32)
        s_nodes[1, k] = window(
            [
                jnp.where(
                    first, shifted(higher[k // 4][c], -(k % 4)), mine[GROUP * c : GROUP * (c + 1)]
                )
                for c in range(3)
            ]
        )
    both = jnp.concatenate([stress_window(1, 0), stress_window(1, 1)], axis=0)
    at = dot(jnp.concatenate([ahead[4], ahead[4]], axis=1), both).astype(BF16)
    into_dflux([at[:, column(c)] for c in range(6)])
    upper = dot(back[1, :, 256:], dflux[...])

    @pl.when(has_below)
    def _():
        up_share.wait_recv()

    from_below = cup_recv[...].astype(F32)[0:GROUP]
    for i in range(3):
        even, odd = around(upper, i)
        arrived = shifted(from_below, -i)
        shares[GROUP * 2 * i : GROUP * (2 * i + 1)] += jnp.where(first, arrived[:, 0:LANES], even)
        shares[GROUP * (2 * i + 1) : GROUP * (2 * i + 2)] += jnp.where(first, arrived[:, LANES:], odd)
    for k in range(8):
        rs_send[k] = raised(shares[56 * k : 56 * (k + 1)], 64)

    def share_copy(off):
        peer = lax.rem(mode + off, modes)
        return remote(
            rs_send.at[peer], rs_recv.at[off], rs_ssem.at[off], rs_rsem.at[off], (dom, peer)
        )

    for off in range(1, modes):
        share_copy(off).start()

    loads[5].wait()
    start_mass = jnp.where(first, jnp.where(has_below, 1.0, 2.0).astype(F32), jnp.ones((GROUP, LANES), F32))
    end_mass = jnp.where(has_above, 1.0, 0.0).astype(F32)

    def project(j, _):
        for i in range(3):
            cols = pl.ds(pl.multiple_of((3 * j + i) * LANES, LANES), LANES)
            mine, over = [], []
            for c in range(3):
                rows = slice(GROUP * c, GROUP * (c + 1))
                upper = grads[1, rows, cols]
                mine.append(grads[0, rows, cols] + jnp.where(first, grads[2, rows, cols] * inside, upper))
                over.append(grads[3, rows, cols] + upper)
            results = []
            for parts, scale in ((mine, start_mass), (over, end_mass)):
                even = (parts[0] + pltpu.roll(parts[2], 1, axis=1)) * (inv_mass[0] * scale)
                odd = parts[1] * (inv_mass[1] * scale)
                results.append([even, odd, pltpu.roll(even, LANES - 1, axis=1)])
            p_nodes[0, 3 * i + j] = window(results[0])
            p_nodes[1, 3 * i + j] = window(
                [jnp.where(first, results[1][c], results[0][c]) for c in range(3)]
            )
        return 0

    lax.fori_loop(0, 3, project, 0)

    def projected_points(layer):
        for i in range(3):
            nodes = jnp.concatenate([p_nodes[layer, 3 * i + j] for j in range(3)], axis=1)
            here = dot(ahead[4 * layer], nodes)
            for j in range(3):
                g_points[layer, 3 * i + j] = here[:, column(j)]

    projected_points(1)
    velocity_points(1, dot(ahead[4], side(v_nodes, 1, 3)))

    def residual_of(layer, m):
        lam = jnp.full((16, LANES), relax[2 * mode + m], F32)
        eta = jnp.full((16, LANES), viscosity[2 * mode + m], F32)
        eps = jnp.full((16, LANES), extension[2 * mode + m], F32)
        half = 0.5 / lam
        slope = 0.5 * eps / eta
        kappa = eta / lam

        def chunk(start):
            rows = pl.ds(start, 16)
            t = [t_points[layer, m, 0, rows, column(c)] for c in range(6)]
            g = [[g_points[layer, 3 * i + j, rows] for j in range(3)] for i in range(3)]
            u = [flow[layer, i, rows] for i in range(3)]
            y = half + slope * (t[0] + t[1] + t[2])
            shift = (y * kappa) * 2.0
            tt = [t[0] + kappa, t[1] + kappa, t[2] + kappa] + t[3:]
            h = [g[k][k] - y for k in range(3)]

            def entry(i, j):
                return tt[SLOT[i][j]]

            for c, (i, j) in enumerate(((0, 0), (1, 1), (2, 2), (0, 1), (0, 2), (1, 2))):
                value = u[0] * t_points[layer, m, 1, rows, column(c)]
                value = value + u[1] * t_points[layer, m, 2, rows, column(c)]
                value = value + u[2] * t_points[layer, m, 3, rows, column(c)]
                if i == j:
                    k, l = (i + 1) % 3, (i + 2) % 3
                    part = h[i] * entry(i, i) + g[i][k] * entry(k, i) + g[i][l] * entry(l, i)
                    value = value - (part + part) - shift
                else:
                    k = 3 - i - j
                    part = (h[i] + h[j]) * entry(i, j)
                    part = part + g[i][j] * entry(j, j) + g[i][k] * entry(k, j)
                    part = part + g[j][i] * entry(i, i) + g[j][k] * entry(k, i)
                    value = value - part
                rounded = value.astype(BF16)
                flux[rows, column(c)] = rounded
                for j2 in range(3):
                    place = pl.ds(256 * (1 + j2) + start, 16)
                    flux[place, column(c)] = rounded * winds[layer, j2, rows]

        def step(k, _):
            chunk(pl.multiple_of(16 * k, 16))
            return 0

        lax.fori_loop(0, POINTS // 16, step, 0, unroll=True)
        sums[layer, m] = dot(back[layer], flux[...])

    weight = viscosity[0]
    for k in range(1, 2 * modes):
        weight = weight + viscosity[k]
    weight = weight * (1.0 / (2 * modes))

    def devss_of(layer):
        values = [None] * 6
        for i in range(3):
            for j in range(i, 3):
                d_ij = derivs[layer, 0:POINTS, column(3 * j + i)].astype(F32)
                d_ji = derivs[layer, 0:POINTS, column(3 * i + j)].astype(F32)
                excess = d_ij + d_ji - g_points[layer, 3 * i + j] - g_points[layer, 3 * j + i]
                values[SLOT[i][j]] = (weight * excess).astype(BF16)
        into_dflux(values)
        devss[layer] = dot(back[layer, :, 256:], dflux[...])

    tops = [
        remote(top_send.at[k], top_recv.at[k], top_ssem.at[k], top_rsem.at[k], above) for k in range(4)
    ]

    points_of(1)
    devss_of(1)
    for m in range(2):
        residual_of(1, m)
        result = sums[1, m]
        blocks = [jnp.concatenate(around(result, c), axis=1) for c in range(6)]
        result = devss[1]
        for i in ((0, 1), (2,))[m]:
            blocks.append(jnp.concatenate(around(result, i), axis=1))
        top_send[2 * m] = raised(packed(blocks[0:4]), SENT)
        top_send[2 * m + 1] = raised(packed(blocks[4:]), SENT)

        @pl.when(has_above)
        def _():
            tops[2 * m].start()
            tops[2 * m + 1].start()

    def sum_shares():
        place = pl.ds(pl.multiple_of(mode * 56, 8), 56)
        total = jnp.concatenate([shares[place], jnp.zeros((8, LANES), F32)], axis=0)
        for off in range(1, modes):
            share_copy(off).wait_recv()
            total = total + rs_recv[off].astype(F32)
        ag_buf[mode] = total.astype(BF16)

    def whole_copy(off, place):
        peer = lax.rem(mode + off, modes)
        return remote(
            ag_buf.at[place], ag_buf.at[place], ag_ssem.at[off], ag_rsem.at[off], (dom, peer)
        )

    sum_shares()
    for off in range(1, modes):
        whole_copy(off, mode).start()

    projected_points(0)
    devss_of(0)
    for m in range(2):
        residual_of(0, m)

    for off in range(1, modes):
        whole_copy(off, lax.rem(mode + modes - off, modes)).wait_recv()

    @pl.when(has_below)
    def _():
        for k in range(4):
            tops[k].wait_recv()

    def nodes_of(lower, upper, c, arrived):
        low = jnp.concatenate(around(lower, c), axis=1)
        high = jnp.concatenate(around(upper, c), axis=1)
        return low + jnp.where(firsts, arrived, high)

    def finish(m, _):
        lam = relax[2 * mode + m]
        lower, upper = sums[0, m], sums[1, m]
        arrived = [top_recv[2 * m + k].astype(F32)[0:GROUP] for k in range(2)]
        for c in range(6):
            both = nodes_of(lower, upper, c, shifted(arrived[c // 4], -(c % 4)))
            pieces[6 * m + c] = raised(both * lam, SENT)
        return 0

    lax.fori_loop(0, 2, finish, 0)

    for k in range(8):
        shares[56 * k : 56 * (k + 1)] = ag_buf[k].astype(F32)[0:56]
    lower, upper = devss[0], devss[1]
    for i in range(3):
        group, place = ((1, 2), (1, 3), (3, 2))[i]
        arrived = shifted(top_recv[group].astype(F32)[0:GROUP], -place)
        both = nodes_of(lower, upper, i, arrived)
        both = both + jnp.concatenate(
            [
                shares[GROUP * 2 * i : GROUP * (2 * i + 1)],
                shares[GROUP * (2 * i + 1) : GROUP * (2 * i + 2)],
            ],
            axis=1,
        )
        rounded = both.astype(BF16).astype(F32)
        pieces[12 + i] = raised(rounded, SENT)
        pieces[15 + i] = raised(both - rounded, SENT)

    @pl.when(has_below)
    def _():
        down_velocity.wait_send()
        down_stress.wait_send()

    @pl.when(has_above)
    def _():
        up_velocity.wait_send()
        up_share.wait_send()
        for k in range(4):
            tops[k].wait_send()

    for off in range(1, modes):
        share_copy(off).wait_send()
        whole_copy(off, mode).wait_send()


def finish_kernel(pieces, merge, out_stress, out_div):
    def merged(k):
        rows = dot(pieces[k], merge[...])[0 : OWN * NODES]
        return rows.reshape(NODES, OWN, 2 * LANES)

    for k in range(12):
        out_stress[k // 6, k % 6] = merged(k).astype(BF16)
    for i in range(3):
        out_div[i] = merged(12 + i) + merged(15 + i)


def on_device(doms, modes, velocity, stress, relax_time, viscosity, extensibility):
    ahead, back = column_tables()
    split, merge = order_tables()
    velocity = jnp.transpose(velocity, (0, 2, 1, 3))
    stress = jnp.transpose(stress, (0, 1, 3, 2, 4))
    vmem = pl.BlockSpec(memory_space=pltpu.VMEM)
    smem = pl.BlockSpec(memory_space=pltpu.SMEM)
    hbm = pl.BlockSpec(memory_space=pltpu.HBM)
    dma = pltpu.SemaphoreType.DMA
    around_nodes = 2 * LANES
    scratch = [
        pltpu.VMEM(velocity.shape, BF16),
        pltpu.VMEM(stress.shape, BF16),
        pltpu.VMEM(ahead.shape, BF16),
        pltpu.VMEM(back.shape, BF16),
        pltpu.VMEM(split.shape, BF16),
        pltpu.VMEM((2, GROUP, LANES), F32),
        pltpu.VMEM((12, SENT, around_nodes), BF16),
        pltpu.VMEM((3, SENT, around_nodes), BF16),
        pltpu.VMEM(velocity.shape, BF16),
        pltpu.VMEM(velocity.shape, BF16),
        pltpu.VMEM((3, SENT, around_nodes), BF16),
        pltpu.VMEM((SENT, around_nodes), BF16),
        pltpu.VMEM((SENT, around_nodes), BF16),
        pltpu.VMEM((4, SENT, around_nodes), BF16),
        pltpu.VMEM((4, SENT, around_nodes), BF16),
        pltpu.VMEM((2, 12, WINDOW, LANES), BF16),
        pltpu.VMEM((4, 3, WINDOW, LANES), BF16),
        pltpu.VMEM((2, 9, WINDOW, LANES), BF16),
        pltpu.VMEM((2, 2, 4, POINTS, 6 * LANES), F32),
        pltpu.VMEM((4 * 256, 6 * LANES), BF16),
        pltpu.VMEM((3 * 256, 3 * LANES), BF16),
        pltpu.VMEM((4, 256, 9 * LANES), BF16),
        pltpu.VMEM((4, COLUMN, 9 * LANES), F32),
        pltpu.VMEM((2, 3, POINTS, LANES), F32),
        pltpu.VMEM((2, 3, POINTS, LANES), BF16),
        pltpu.VMEM((2, 9, POINTS, LANES), F32),
        pltpu.VMEM((2, 2, COLUMN, 6 * LANES), F32),
        pltpu.VMEM((2, COLUMN, 3 * LANES), F32),
        pltpu.VMEM((448, LANES), F32),
        pltpu.VMEM((8, 64, LANES), BF16),
        pltpu.VMEM((8, 64, LANES), BF16),
        pltpu.VMEM((8, 64, LANES), BF16),
        dma((6,)),
        dma((4,)),
        dma((4,)),
        dma((modes,)),
        dma((modes,)),
        dma((modes,)),
        dma((modes,)),
        dma((4,)),
        dma((4,)),
    ]
    pieces = pl.pallas_call(
        functools.partial(kernel, doms, modes),
        out_shape=pltpu.VMEM((18, SENT, around_nodes), BF16),
        in_specs=[hbm, hbm, smem, smem, smem, hbm, hbm, hbm, hbm],
        out_specs=vmem,
        scratch_shapes=scratch,
        compiler_params=pltpu.CompilerParams(
            collective_id=0, has_side_effects=True, vmem_limit_bytes=58 * 1024 * 1024
        ),
        name="ptt",
    )(
        velocity,
        stress,
        relax_time,
        viscosity,
        extensibility,
        jnp.asarray(ahead),
        jnp.asarray(back),
        jnp.asarray(split),
        jnp.asarray(inverse_mass()),
    )
    out_stress, out_div = pl.pallas_call(
        finish_kernel,
        out_shape=(
            jax.ShapeDtypeStruct(stress.shape, BF16),
            jax.ShapeDtypeStruct(velocity.shape, F32),
        ),
        in_specs=[vmem, vmem],
        out_specs=(vmem, vmem),
        compiler_params=pltpu.CompilerParams(vmem_limit_bytes=16 * 1024 * 1024),
        name="finish",
    )(pieces, jnp.asarray(merge))
    return jnp.transpose(out_stress, (0, 1, 3, 2, 4)), jnp.transpose(out_div, (0, 2, 1, 3))


def solution(mesh):
    return jax.shard_map(
        functools.partial(on_device, mesh.shape["dom"], mesh.shape["mode"]),
        mesh=mesh,
        in_specs=(P(None, "dom", None, None), P("mode", None, "dom", None, None), P(), P(), P()),
        out_specs=(P("mode", None, "dom", None, None), P(None, "dom", None, None)),
        check_vma=False,
    )
```

time: 33.8 us -> 26.7 us (0.79)
  local copies, waits for them, and re-layouts: 3.87 us -> 0.01 us
  Pallas kernels: 29 us -> 25.9 us
    pallas_call x1 -> x2, Pallas kernels: 29 us -> 25.9 us  [the longest x1 24.6 us: on_device(): pl.pallas_call(functools.partial(kernel, doms, modes), out_shape=pltpu.VM...]
    unnamed x18 -> x2, local copies, waits for them, and re-layouts: 2.19 us -> 0.01 us
    pallas_call x2 -> x0, local copies, waits for them, and re-layouts: 1.68 us -> none  [on_device(): pl.pallas_call(functools.partial(kernel, doms, modes), out_shape=(jax.Sha...]
where the time goes in v1:
time: 26.7 us; the launch traced here: 26.6 us
  Pallas kernels  25.9 us (97%)
  between operations  0.65 us (2%)
    pallas_call x1, Pallas kernels, on_device(): pl.pallas_call(functools.partial(kernel, doms, modes), out_shape=pltpu.VM...  24.6 us
    pallas_call x1, Pallas kernels, on_device(): pl.pallas_call(finish_kernel, out_shape=(jax.ShapeDtypeStruct(stress.shap...  1.25 us

profile of v1, /device:TPU:384, one launch (start us, length us, event | category | flops | bytes accessed | tf_op | source)
XLA Modules:
  0.0 26.6 jit_solution(68338078100691453)
XLA Ops:
  0.6 0.0 copy-start
  0.6 24.6 %ptt.1.pieces = bf16[18,80,256]{2,1,0:T(8,128)(2,1)S(1)} custom-call(bf16[3,17,4,256]{3,2,1,0:T(4,128)(2,1)} %bitcast.5, bf16[2,6,17,4,256]{4,3,2,1,0:T(4,128)(2,1)} %bitcast.4, f32[16]{0:T(128)} %relax.1, f32[16]{0:T(128)} %viscosity.1, f32[16]{0:T(128)} %extension.1, bf16[10,224,256]{2,1,0:T(8,128)(2,1)} %constant.10.clone.ahead_hbm, ...), custom_call_target="tpu_custom_call" | custom-call | tf_op jit(solution)/shard_map/ptt/pallas_call | solution.py:691
  25.3 0.0 copy-done
  25.3 1.2 %finish.1 = (bf16[2,6,17,4,256]{4,3,2,1,0:T(4,128)(2,1)}, f32[3,17,4,256]{3,2,1,0:T(4,128)}) custom-call(bf16[18,80,256]{2,1,0:T(8,128)(2,1)S(1)} %ptt.1.pieces, bf16[256,256]{1,0:T(8,128)(2,1)S(1)} %copy-done), custom_call_target="tpu_custom_call" | custom-call | tf_op jit(solution)/shard_map/finish/pallas_call | solution.py:712
Async XLA Ops:
  0.6 24.7 %copy-start = (bf16[256,256]{1,0:T(8,128)(2,1)S(1)}, bf16[256,256]{1,0:T(8,128)(2,1)}, u32[]{:S(2)}) copy-start(bf16[256,256]{1,0:T(8,128)(2,1)} %constant.14.clone.merge) | copy-start | bytes 393220

commit v2 on v1

--- a/solution.py
+++ b/solution.py
@@ -136,6 +136,7 @@
     t_points,
     flux,
     dflux,
+    masked,
     derivs,
     grads,
     flow,
@@ -180,14 +181,23 @@
         pl.semaphore_signal(barrier, inc=1, device_id=(dom, peer), device_id_type=MESH)
 
     pairs = (
+        (stress_hbm.at[0], stress.at[0]),
+        (stress_hbm.at[1], stress.at[1]),
+        (split_hbm, split),
+        (ahead_hbm.at[pl.ds(8, 2)], ahead.at[pl.ds(8, 2)]),
+        (ahead_hbm.at[pl.ds(0, 4)], ahead.at[pl.ds(0, 4)]),
+        (back_hbm.at[1], back.at[1]),
+        (back_hbm.at[0], back.at[0]),
         (velocity_hbm, velocity),
-        (stress_hbm, stress),
-        (split_hbm, split),
-        (ahead_hbm, ahead),
-        (back_hbm, back),
+        (ahead_hbm.at[pl.ds(4, 4)], ahead.at[pl.ds(4, 4)]),
         (mass_hbm, inv_mass),
     )
     loads = [pltpu.make_async_copy(a, b, local_sem.at[k]) for k, (a, b) in enumerate(pairs)]
+
+    def arrived_here(*which):
+        for k in which:
+            loads[k].wait()
+
     for load in loads:
         load.start()
 
@@ -237,7 +247,7 @@
             axis=0,
         )
 
-    loads[1].wait()
+    arrived_here(0, 1)
     for g in range(3):
         blocks = []
         for q in range(4):
@@ -258,10 +268,10 @@
     for d in range(4):
         flux[256 * d + POINTS : 256 * (d + 1)] = jnp.zeros((256 - POINTS, 6 * LANES), BF16)
         derivs[d, POINTS:] = jnp.zeros((256 - POINTS, 9 * LANES), BF16)
-    for d in range(3):
+    for d in range(9):
         dflux[256 * d + POINTS : 256 * (d + 1)] = jnp.zeros((256 - POINTS, 3 * LANES), BF16)
 
-    loads[2].wait()
+    arrived_here(2)
     for k in range(4):
         own = laid_out([s_rows[3 * k + c] for c in range(3)])
         for c in range(3):
@@ -277,21 +287,13 @@
         even = result[0:GROUP, column(c)] + pltpu.roll(result[2 * GROUP :, column(c)], 1, axis=1)
         return even, result[GROUP : 2 * GROUP, column(c)]
 
-    def points_of(layer):
-        for m in range(2):
-            nodes = stress_window(layer, m)
-            for d in range(4):
-                t_points[layer, m, d] = dot(ahead[4 * layer + d], nodes)
-
-    def into_dflux(values):
+    def points_of(layer, m, d):
+        t_points[layer, m, d] = dot(ahead[4 * layer + d], stress_window(layer, m))
+
+    def into(ref, values):
         for j in range(3):
             for i in range(3):
-                dflux[256 * j : 256 * j + POINTS, column(i)] = values[SLOT[i][j]]
-
-    loads[0].wait()
-    own_velocity = laid_out([raised(rows_of(velocity[i]), SENT) for i in range(3)])
-    for i in range(3):
-        v_nodes[0, i] = window(own_velocity[i])
+                ref[256 * j : 256 * j + POINTS, column(i)] = values[SLOT[i][j]]
 
     others = modes - 1 + has_below.astype(jnp.int32) + has_above.astype(jnp.int32)
     pl.semaphore_wait(barrier, others)
@@ -299,44 +301,45 @@
     @pl.when(has_below)
     def _():
         down_velocity.start()
+
+    @pl.when(has_above)
+    def _():
+        up_velocity.start()
+
+    @pl.when(has_below)
+    def _():
         down_stress.start()
 
+    arrived_here(3, 4, 5, 6)
+    both = jnp.concatenate([stress_window(0, 0), stress_window(0, 1)], axis=0)
+    parts = jnp.concatenate([ahead[8], ahead[9], ahead[0]], axis=0)
+    at = dot(jnp.concatenate([parts, parts], axis=1), both)
+    for part in range(3):
+        here = at[POINTS * part : POINTS * (part + 1)]
+        if part == 1:
+            here = here * inside
+        here = here.astype(BF16)
+        into(dflux.at[pl.ds(768 * part, 768)], [here[:, column(c)] for c in range(6)])
+    outer = dot(back[1, :, 256:], dflux[0:768])
+    for k in range(3):
+        rows = slice(GROUP * k, GROUP * (k + 1))
+        own = back[1, rows].astype(F32)
+        zero = jnp.zeros_like(own)
+        is_first = jnp.concatenate([first] * 8, axis=1)
+        masked[0, rows] = jnp.where(is_first, own, zero)
+        masked[1, rows] = jnp.where(is_first, zero, own[:, 0:1024])
+    tested = jnp.concatenate([masked[0, :, 256:].astype(BF16), back[0, :, 256:]], axis=1)
+    local = dot(tested, dflux[768:])
+    cup_send[...] = raised(packed([jnp.concatenate(around(outer, i), axis=1) for i in range(3)]), SENT)
+
     @pl.when(has_above)
     def _():
-        up_velocity.start()
-
-    loads[3].wait()
-    loads[4].wait()
-    both = jnp.concatenate([stress_window(0, 0), stress_window(0, 1)], axis=0)
-
-    def outer_share(part):
-        at = dot(jnp.concatenate([part, part], axis=1), both).astype(BF16)
-        into_dflux([at[:, column(c)] for c in range(6)])
-        return dot(back[1, :, 256:], dflux[...])
-
-    outer = outer_share(ahead[8])
-    cup_send[...] = raised(packed([jnp.concatenate(around(outer, i), axis=1) for i in range(3)]), SENT)
-
-    @pl.when(has_above)
-    def _():
         up_share.start()
 
-    outer = outer_share(ahead[9])
     for i in range(3):
-        even, odd = around(outer, i)
-        zero = jnp.zeros_like(even)
-        shares[GROUP * 2 * i : GROUP * (2 * i + 1)] = jnp.where(first, even * inside, zero)
-        shares[GROUP * (2 * i + 1) : GROUP * (2 * i + 2)] = jnp.where(first, odd * inside, zero)
-
-    def add_shares(result):
-        for i in range(3):
-            even, odd = around(result, i)
-            shares[GROUP * 2 * i : GROUP * (2 * i + 1)] += even
-            shares[GROUP * (2 * i + 1) : GROUP * (2 * i + 2)] += odd
-
-    at = dot(jnp.concatenate([ahead[0], ahead[0]], axis=1), both).astype(BF16)
-    into_dflux([at[:, column(c)] for c in range(6)])
-    add_shares(dot(back[0, :, 256:], dflux[...]))
+        even, odd = around(local, i)
+        shares[GROUP * 2 * i : GROUP * (2 * i + 1)] = even
+        shares[GROUP * (2 * i + 1) : GROUP * (2 * i + 2)] = odd
 
     def velocity_points(layer, at):
         at = at.astype(BF16).astype(F32)
@@ -351,11 +354,14 @@
         for j in range(3):
             at = dot(ahead[4 * layer + 1 + j], nodes)
             derivs[variant, 0:POINTS, 3 * LANES * j : 3 * LANES * (j + 1)] = at.astype(BF16)
-        grads[variant] = dot(back[layer, :, 0:256], derivs[variant])
+
+    arrived_here(7)
+    own_velocity = laid_out([raised(rows_of(velocity[i]), SENT) for i in range(3)])
+    for i in range(3):
+        v_nodes[0, i] = window(own_velocity[i])
 
     velocity_points(0, dot(ahead[0], side(v_nodes, 0, 3)))
     gradient_points(0, 0)
-    points_of(0)
 
     @pl.when(has_above)
     def _():
@@ -373,11 +379,18 @@
     ]
     for i in range(3):
         v_nodes[1, i] = window([jnp.where(first, higher[i][c], own[i][c]) for c in range(3)])
-        v_nodes[2, i] = window([jnp.where(first, own[i][c], lower[i][c]) for c in range(3)])
+        v_nodes[2, i] = window([jnp.where(first, own[i][c] * inside, lower[i][c]) for c in range(3)])
         v_nodes[3, i] = window(higher[i])
+    arrived_here(8)
     gradient_points(1, 1)
     gradient_points(2, 1)
     gradient_points(3, 0)
+    tested = jnp.concatenate(
+        [back[0, :, 0:256], masked[1, :, 0:256].astype(BF16), masked[0, :, 0:256].astype(BF16)], axis=1
+    )
+    grads[0] = dot(tested, jnp.concatenate([derivs[0], derivs[1], derivs[2]], axis=0))
+    tested = jnp.concatenate([back[1, :, 0:256], back[0, :, 0:256]], axis=1)
+    grads[1] = dot(tested, jnp.concatenate([derivs[1], derivs[3]], axis=0))
 
     @pl.when(has_above)
     def _():
@@ -396,8 +409,8 @@
         )
     both = jnp.concatenate([stress_window(1, 0), stress_window(1, 1)], axis=0)
     at = dot(jnp.concatenate([ahead[4], ahead[4]], axis=1), both).astype(BF16)
-    into_dflux([at[:, column(c)] for c in range(6)])
-    upper = dot(back[1, :, 256:], dflux[...])
+    into(dflux.at[pl.ds(0, 768)], [at[:, column(c)] for c in range(6)])
+    upper = dot(back[1, :, 256:], dflux[0:768])
 
     @pl.when(has_below)
     def _():
@@ -421,7 +434,7 @@
     for off in range(1, modes):
         share_copy(off).start()
 
-    loads[5].wait()
+    arrived_here(9)
     start_mass = jnp.where(first, jnp.where(has_below, 1.0, 2.0).astype(F32), jnp.ones((GROUP, LANES), F32))
     end_mass = jnp.where(has_above, 1.0, 0.0).astype(F32)
 
@@ -431,9 +444,8 @@
             mine, over = [], []
             for c in range(3):
                 rows = slice(GROUP * c, GROUP * (c + 1))
-                upper = grads[1, rows, cols]
-                mine.append(grads[0, rows, cols] + jnp.where(first, grads[2, rows, cols] * inside, upper))
-                over.append(grads[3, rows, cols] + upper)
+                mine.append(grads[0, rows, cols])
+                over.append(grads[1, rows, cols])
             results = []
             for parts, scale in ((mine, start_mass), (over, end_mass)):
                 even = (parts[0] + pltpu.roll(parts[2], 1, axis=1)) * (inv_mass[0] * scale)
@@ -457,7 +469,7 @@
     projected_points(1)
     velocity_points(1, dot(ahead[4], side(v_nodes, 1, 3)))
 
-    def residual_of(layer, m):
+    def residual_of(layer, m, following):
         lam = jnp.full((16, LANES), relax[2 * mode + m], F32)
         eta = jnp.full((16, LANES), viscosity[2 * mode + m], F32)
         eps = jnp.full((16, LANES), extension[2 * mode + m], F32)
@@ -502,7 +514,11 @@
             chunk(pl.multiple_of(16 * k, 16))
             return 0
 
-        lax.fori_loop(0, POINTS // 16, step, 0, unroll=True)
+        bounds = (0, 4, 8, 11, 14)
+        for d in range(4):
+            lax.fori_loop(bounds[d], bounds[d + 1], step, 0, unroll=True)
+            if following is not None:
+                points_of(*following, d)
         sums[layer, m] = dot(back[layer], flux[...])
 
     weight = viscosity[0]
@@ -518,17 +534,18 @@
                 d_ji = derivs[layer, 0:POINTS, column(3 * i + j)].astype(F32)
                 excess = d_ij + d_ji - g_points[layer, 3 * i + j] - g_points[layer, 3 * j + i]
                 values[SLOT[i][j]] = (weight * excess).astype(BF16)
-        into_dflux(values)
-        devss[layer] = dot(back[layer, :, 256:], dflux[...])
+        into(dflux.at[pl.ds(0, 768)], values)
+        devss[layer] = dot(back[layer, :, 256:], dflux[0:768])
 
     tops = [
         remote(top_send.at[k], top_recv.at[k], top_ssem.at[k], top_rsem.at[k], above) for k in range(4)
     ]
 
-    points_of(1)
+    for d in range(4):
+        points_of(1, 0, d)
     devss_of(1)
     for m in range(2):
-        residual_of(1, m)
+        residual_of(1, m, ((1, 1), (0, 0))[m])
         result = sums[1, m]
         blocks = [jnp.concatenate(around(result, c), axis=1) for c in range(6)]
         result = devss[1]
@@ -563,10 +580,7 @@
     projected_points(0)
     devss_of(0)
     for m in range(2):
-        residual_of(0, m)
-
-    for off in range(1, modes):
-        whole_copy(off, lax.rem(mode + modes - off, modes)).wait_recv()
+        residual_of(0, m, ((0, 1), None)[m])
 
     @pl.when(has_below)
     def _():
@@ -588,6 +602,9 @@
         return 0
 
     lax.fori_loop(0, 2, finish, 0)
+
+    for off in range(1, modes):
+        whole_copy(off, lax.rem(mode + modes - off, modes)).wait_recv()
 
     for k in range(8):
         shares[56 * k : 56 * (k + 1)] = ag_buf[k].astype(F32)[0:56]
@@ -624,15 +641,26 @@
         whole_copy(off, mode).wait_send()
 
 
-def finish_kernel(pieces, merge, out_stress, out_div):
-    def merged(k):
-        rows = dot(pieces[k], merge[...])[0 : OWN * NODES]
-        return rows.reshape(NODES, OWN, 2 * LANES)
-
-    for k in range(12):
-        out_stress[k // 6, k % 6] = merged(k).astype(BF16)
-    for i in range(3):
-        out_div[i] = merged(12 + i) + merged(15 + i)
+def finish_kernel(pieces, merge, out_stress, out_div, stress_rows, div_rows, sem):
+    def merged(first):
+        rows = dot(jnp.concatenate([pieces[first + k] for k in range(3)], axis=0), merge[...])
+        return [
+            rows[SENT * k : SENT * k + OWN * NODES].reshape(NODES, OWN, 2 * LANES) for k in range(3)
+        ]
+
+    copies = []
+    for g in range(4):
+        place = (g // 2, pl.ds(3 * (g % 2), 3))
+        for k, rows in enumerate(merged(3 * g)):
+            stress_rows[g // 2, 3 * (g % 2) + k] = rows.astype(BF16)
+        copies.append(pltpu.make_async_copy(stress_rows.at[place], out_stress.at[place], sem.at[g]))
+        copies[g].start()
+    for k, (high, low) in enumerate(zip(merged(12), merged(15))):
+        div_rows[k] = high + low
+    copies.append(pltpu.make_async_copy(div_rows, out_div, sem.at[4]))
+    copies[4].start()
+    for copy in copies:
+        copy.wait()
 
 
 def on_device(doms, modes, velocity, stress, relax_time, viscosity, extensibility):
@@ -666,9 +694,10 @@
         pltpu.VMEM((2, 9, WINDOW, LANES), BF16),
         pltpu.VMEM((2, 2, 4, POINTS, 6 * LANES), F32),
         pltpu.VMEM((4 * 256, 6 * LANES), BF16),
-        pltpu.VMEM((3 * 256, 3 * LANES), BF16),
+        pltpu.VMEM((9 * 256, 3 * LANES), BF16),
+        pltpu.VMEM((2, COLUMN, 4 * 256), F32),
         pltpu.VMEM((4, 256, 9 * LANES), BF16),
-        pltpu.VMEM((4, COLUMN, 9 * LANES), F32),
+        pltpu.VMEM((2, COLUMN, 9 * LANES), F32),
         pltpu.VMEM((2, 3, POINTS, LANES), F32),
         pltpu.VMEM((2, 3, POINTS, LANES), BF16),
         pltpu.VMEM((2, 9, POINTS, LANES), F32),
@@ -678,7 +707,7 @@
         pltpu.VMEM((8, 64, LANES), BF16),
         pltpu.VMEM((8, 64, LANES), BF16),
         pltpu.VMEM((8, 64, LANES), BF16),
-        dma((6,)),
+        dma((10,)),
         dma((4,)),
         dma((4,)),
         dma((modes,)),
@@ -716,7 +745,8 @@
             jax.ShapeDtypeStruct(velocity.shape, F32),
         ),
         in_specs=[vmem, vmem],
-        out_specs=(vmem, vmem),
+        out_specs=(hbm, hbm),
+        scratch_shapes=[pltpu.VMEM(stress.shape, BF16), pltpu.VMEM(velocity.shape, F32), dma((5,))],
         compiler_params=pltpu.CompilerParams(vmem_limit_bytes=16 * 1024 * 1024),
         name="finish",
     )(pieces, jnp.asarray(merge))

time: 26.7 us -> 26.4 us (0.989)
  Pallas kernels: 25.9 us -> 25.6 us
where the time goes in v2:
time: 26.4 us; the launch traced here: 26.3 us
  Pallas kernels  25.6 us (97%)
  between operations  0.65 us (2%)
    pallas_call x1, Pallas kernels, on_device(): pl.pallas_call(functools.partial(kernel, doms, modes), out_shape=pltpu.VM...  24.5 us
    pallas_call x1, Pallas kernels, on_device(): pl.pallas_call(finish_kernel, out_shape=(jax.ShapeDtypeStruct(stress.shap...  1.1 us

profile of v2, /device:TPU:384, one launch (start us, length us, event | category | flops | bytes accessed | tf_op | source)
XLA Modules:
  0.0 26.3 jit_solution(352268910357747608)
XLA Ops:
  0.6 0.0 copy-start
  0.6 24.5 %ptt.1.pieces = bf16[18,80,256]{2,1,0:T(8,128)(2,1)S(1)} custom-call(bf16[3,17,4,256]{3,2,1,0:T(4,128)(2,1)} %bitcast.5, bf16[2,6,17,4,256]{4,3,2,1,0:T(4,128)(2,1)} %bitcast.4, f32[16]{0:T(128)} %relax.1, f32[16]{0:T(128)} %viscosity.1, f32[16]{0:T(128)} %extension.1, bf16[10,224,256]{2,1,0:T(8,128)(2,1)} %constant.10.clone.ahead_hbm, ...), custom_call_target="tpu_custom_call" | custom-call | tf_op jit(solution)/shard_map/ptt/pallas_call | solution.py:720
  25.2 0.0 copy-done
  25.2 1.1 %finish.1 = (bf16[2,6,17,4,256]{4,3,2,1,0:T(4,128)(2,1)}, f32[3,17,4,256]{3,2,1,0:T(4,128)}) custom-call(bf16[18,80,256]{2,1,0:T(8,128)(2,1)S(1)} %ptt.1.pieces, bf16[256,256]{1,0:T(8,128)(2,1)S(1)} %copy-done), custom_call_target="tpu_custom_call" | custom-call | tf_op jit(solution)/shard_map/finish/pallas_call | solution.py:741
Async XLA Ops:
  0.6 24.5 %copy-start = (bf16[256,256]{1,0:T(8,128)(2,1)S(1)}, bf16[256,256]{1,0:T(8,128)(2,1)}, u32[]{:S(2)}) copy-start(bf16[256,256]{1,0:T(8,128)(2,1)} %constant.14.clone.merge) | copy-start | bytes 393220

commit v3 on v2

--- a/solution.py
+++ b/solution.py
@@ -64,11 +64,7 @@
                     rows = slice(27 * d, 27 * d + 27)
                     ahead[layer, d, 27 * f : 27 * f + 27, node] = forward[rows, n]
                     back[layer, node, 256 * d + 27 * f : 256 * d + 27 * f + 27] = testing[n, rows]
-    first = np.arange(WINDOW) % OWN == 0
-    parts = np.zeros((2, POINTS, WINDOW), np.float32)
-    parts[0] = ahead[1, 0] * ~first
-    parts[1] = ahead[1, 0] * first
-    ahead = np.concatenate([ahead.reshape(8, POINTS, WINDOW), parts])
+    ahead = ahead.reshape(8, POINTS, WINDOW)
     return ahead.astype(ml_dtypes.bfloat16), back.astype(ml_dtypes.bfloat16)
 
 
@@ -184,12 +180,13 @@
         (stress_hbm.at[0], stress.at[0]),
         (stress_hbm.at[1], stress.at[1]),
         (split_hbm, split),
-        (ahead_hbm.at[pl.ds(8, 2)], ahead.at[pl.ds(8, 2)]),
-        (ahead_hbm.at[pl.ds(0, 4)], ahead.at[pl.ds(0, 4)]),
+        (ahead_hbm.at[0], ahead.at[0]),
+        (ahead_hbm.at[4], ahead.at[4]),
         (back_hbm.at[1], back.at[1]),
         (back_hbm.at[0], back.at[0]),
         (velocity_hbm, velocity),
-        (ahead_hbm.at[pl.ds(4, 4)], ahead.at[pl.ds(4, 4)]),
+        (ahead_hbm.at[pl.ds(1, 3)], ahead.at[pl.ds(1, 3)]),
+        (ahead_hbm.at[pl.ds(5, 3)], ahead.at[pl.ds(5, 3)]),
         (mass_hbm, inv_mass),
     )
     loads = [pltpu.make_async_copy(a, b, local_sem.at[k]) for k, (a, b) in enumerate(pairs)]
@@ -312,7 +309,17 @@
 
     arrived_here(3, 4, 5, 6)
     both = jnp.concatenate([stress_window(0, 0), stress_window(0, 1)], axis=0)
-    parts = jnp.concatenate([ahead[8], ahead[9], ahead[0]], axis=0)
+    upper = ahead[4].astype(F32)
+    lane = lax.rem(lax.broadcasted_iota(jnp.int32, (POINTS, WINDOW), 1), OWN)
+    zero = jnp.zeros_like(upper)
+    parts = jnp.concatenate(
+        [
+            jnp.where(lane == 0, zero, upper).astype(BF16),
+            jnp.where(lane == 0, upper, zero).astype(BF16),
+            ahead[0],
+        ],
+        axis=0,
+    )
     at = dot(jnp.concatenate([parts, parts], axis=1), both)
     for part in range(3):
         here = at[POINTS * part : POINTS * (part + 1)]
@@ -355,7 +362,7 @@
             at = dot(ahead[4 * layer + 1 + j], nodes)
             derivs[variant, 0:POINTS, 3 * LANES * j : 3 * LANES * (j + 1)] = at.astype(BF16)
 
-    arrived_here(7)
+    arrived_here(7, 8)
     own_velocity = laid_out([raised(rows_of(velocity[i]), SENT) for i in range(3)])
     for i in range(3):
         v_nodes[0, i] = window(own_velocity[i])
@@ -381,7 +388,7 @@
         v_nodes[1, i] = window([jnp.where(first, higher[i][c], own[i][c]) for c in range(3)])
         v_nodes[2, i] = window([jnp.where(first, own[i][c] * inside, lower[i][c]) for c in range(3)])
         v_nodes[3, i] = window(higher[i])
-    arrived_here(8)
+    arrived_here(9)
     gradient_points(1, 1)
     gradient_points(2, 1)
     gradient_points(3, 0)
@@ -434,7 +441,7 @@
     for off in range(1, modes):
         share_copy(off).start()
 
-    arrived_here(9)
+    arrived_here(10)
     start_mass = jnp.where(first, jnp.where(has_below, 1.0, 2.0).astype(F32), jnp.ones((GROUP, LANES), F32))
     end_mass = jnp.where(has_above, 1.0, 0.0).astype(F32)
 
@@ -588,9 +595,14 @@
             tops[k].wait_recv()
 
     def nodes_of(lower, upper, c, arrived):
-        low = jnp.concatenate(around(lower, c), axis=1)
-        high = jnp.concatenate(around(upper, c), axis=1)
-        return low + jnp.where(firsts, arrived, high)
+        parts = []
+        for k in range(3):
+            rows = slice(GROUP * k, GROUP * (k + 1))
+            high = upper[rows, column(c)]
+            parts.append(lower[rows, column(c)] + jnp.where(first, jnp.zeros_like(high), high))
+        even = parts[0] + pltpu.roll(parts[2], 1, axis=1)
+        both = jnp.concatenate([even, parts[1]], axis=1)
+        return both + jnp.where(firsts, arrived, jnp.zeros_like(both))
 
     def finish(m, _):
         lam = relax[2 * mode + m]
@@ -707,7 +719,7 @@
         pltpu.VMEM((8, 64, LANES), BF16),
         pltpu.VMEM((8, 64, LANES), BF16),
         pltpu.VMEM((8, 64, LANES), BF16),
-        dma((10,)),
+        dma((11,)),
         dma((4,)),
         dma((4,)),
         dma((modes,)),

time: 26.4 us -> 26.4 us (level)
  no operation moved by 1% of the time
where the time goes in v3:
time: 26.4 us; the launch traced here: 26.3 us
  Pallas kernels  25.6 us (97%)
  between operations  0.65 us (2%)
    pallas_call x1, Pallas kernels, on_device(): pl.pallas_call(functools.partial(kernel, doms, modes), out_shape=pltpu.VM...  24.5 us
    pallas_call x1, Pallas kernels, on_device(): pl.pallas_call(finish_kernel, out_shape=(jax.ShapeDtypeStruct(stress.shap...  1.1 us

profile of v3, /device:TPU:384, one launch (start us, length us, event | category | flops | bytes accessed | tf_op | source)
XLA Modules:
  0.0 26.3 jit_solution(6529770354452552647)
XLA Ops:
  0.6 0.0 copy-start
  0.6 24.5 %ptt.1.pieces = bf16[18,80,256]{2,1,0:T(8,128)(2,1)S(1)} custom-call(bf16[3,17,4,256]{3,2,1,0:T(4,128)(2,1)} %bitcast.5, bf16[2,6,17,4,256]{4,3,2,1,0:T(4,128)(2,1)} %bitcast.4, f32[16]{0:T(128)} %relax.1, f32[16]{0:T(128)} %viscosity.1, f32[16]{0:T(128)} %extension.1, bf16[8,224,256]{2,1,0:T(8,128)(2,1)} %constant.10.clone.ahead_hbm, ...), custom_call_target="tpu_custom_call" | custom-call | tf_op jit(solution)/shard_map/ptt/pallas_call | solution.py:732
  25.2 0.0 copy-done
  25.2 1.1 %finish.1 = (bf16[2,6,17,4,256]{4,3,2,1,0:T(4,128)(2,1)}, f32[3,17,4,256]{3,2,1,0:T(4,128)}) custom-call(bf16[18,80,256]{2,1,0:T(8,128)(2,1)S(1)} %ptt.1.pieces, bf16[256,256]{1,0:T(8,128)(2,1)S(1)} %copy-done), custom_call_target="tpu_custom_call" | custom-call | tf_op jit(solution)/shard_map/finish/pallas_call | solution.py:753
Async XLA Ops:
  0.6 24.5 %copy-start = (bf16[256,256]{1,0:T(8,128)(2,1)S(1)}, bf16[256,256]{1,0:T(8,128)(2,1)}, u32[]{:S(2)}) copy-start(bf16[256,256]{1,0:T(8,128)(2,1)} %constant.14.clone.merge) | copy-start | bytes 393220

commit v4 on v3

--- a/solution.py
+++ b/solution.py
@@ -119,6 +119,7 @@
     inv_mass,
     s_rows,
     str_down,
+    vel_up,
     vel_above,
     vel_below,
     str_above,
@@ -177,6 +178,7 @@
         pl.semaphore_signal(barrier, inc=1, device_id=(dom, peer), device_id_type=MESH)
 
     pairs = (
+        (velocity_hbm, velocity),
         (stress_hbm.at[0], stress.at[0]),
         (stress_hbm.at[1], stress.at[1]),
         (split_hbm, split),
@@ -184,7 +186,6 @@
         (ahead_hbm.at[4], ahead.at[4]),
         (back_hbm.at[1], back.at[1]),
         (back_hbm.at[0], back.at[0]),
-        (velocity_hbm, velocity),
         (ahead_hbm.at[pl.ds(1, 3)], ahead.at[pl.ds(1, 3)]),
         (ahead_hbm.at[pl.ds(5, 3)], ahead.at[pl.ds(5, 3)]),
         (mass_hbm, inv_mass),
@@ -210,7 +211,7 @@
 
     down_velocity = remote(velocity_hbm, vel_above, halo_send.at[0], halo_recv.at[0], below)
     down_stress = remote(str_down, str_above, halo_send.at[1], halo_recv.at[1], below)
-    up_velocity = remote(velocity_hbm, vel_below, halo_send.at[2], halo_recv.at[2], above)
+    up_velocity = remote(vel_up, vel_below, halo_send.at[2], halo_recv.at[2], above)
     up_share = remote(cup_send, cup_recv, halo_send.at[3], halo_recv.at[3], above)
 
     @pl.when(jnp.logical_not(has_above))
@@ -244,7 +245,11 @@
             axis=0,
         )
 
-    arrived_here(0, 1)
+    arrived_here(0)
+    blocks = [rows_of(velocity[i]) for i in range(3)]
+    vel_up[0] = raised(jnp.where(slots >= 2, blocks[0], shifted(blocks[1], -2)), SENT)
+    vel_up[1] = raised(blocks[2], SENT)
+    arrived_here(1, 2)
     for g in range(3):
         blocks = []
         for q in range(4):
@@ -268,7 +273,7 @@
     for d in range(9):
         dflux[256 * d + POINTS : 256 * (d + 1)] = jnp.zeros((256 - POINTS, 3 * LANES), BF16)
 
-    arrived_here(2)
+    arrived_here(3)
     for k in range(4):
         own = laid_out([s_rows[3 * k + c] for c in range(3)])
         for c in range(3):
@@ -307,7 +312,7 @@
     def _():
         down_stress.start()
 
-    arrived_here(3, 4, 5, 6)
+    arrived_here(4, 5, 6, 7)
     both = jnp.concatenate([stress_window(0, 0), stress_window(0, 1)], axis=0)
     upper = ahead[4].astype(F32)
     lane = lax.rem(lax.broadcasted_iota(jnp.int32, (POINTS, WINDOW), 1), OWN)
@@ -362,7 +367,7 @@
             at = dot(ahead[4 * layer + 1 + j], nodes)
             derivs[variant, 0:POINTS, 3 * LANES * j : 3 * LANES * (j + 1)] = at.astype(BF16)
 
-    arrived_here(7, 8)
+    arrived_here(8)
     own_velocity = laid_out([raised(rows_of(velocity[i]), SENT) for i in range(3)])
     for i in range(3):
         v_nodes[0, i] = window(own_velocity[i])
@@ -378,7 +383,11 @@
     def _():
         up_velocity.wait_recv()
 
-    six = laid_out([raised(rows_of(ref[i]), SENT) for ref in (vel_above, vel_below) for i in range(3)])
+    two = [vel_below[k].astype(F32)[0:GROUP] for k in range(2)]
+    six = laid_out(
+        [raised(rows_of(vel_above[i]), SENT) for i in range(3)]
+        + [raised(b, SENT) for b in (two[0], shifted(two[0], 2), two[1])]
+    )
     higher, lower = six[0:3], six[3:6]
     own = [
         [v_nodes[0, i, 0:224].astype(F32)[GROUP * c : GROUP * (c + 1)] for c in range(3)]
@@ -694,8 +703,9 @@
         pltpu.VMEM((2, GROUP, LANES), F32),
         pltpu.VMEM((12, SENT, around_nodes), BF16),
         pltpu.VMEM((3, SENT, around_nodes), BF16),
+        pltpu.VMEM((2, SENT, around_nodes), BF16),
         pltpu.VMEM(velocity.shape, BF16),
-        pltpu.VMEM(velocity.shape, BF16),
+        pltpu.VMEM((2, SENT, around_nodes), BF16),
         pltpu.VMEM((3, SENT, around_nodes), BF16),
         pltpu.VMEM((SENT, around_nodes), BF16),
         pltpu.VMEM((SENT, around_nodes), BF16),

time: 26.4 us -> 26 us (0.985)
  the two profiles are of different devices: /device:TPU:384 before, /device:TPU:387 now
where the time goes in v4:
time: 26 us; the launch traced here: 25.9 us
  Pallas kernels  25.2 us (97%)
  between operations  0.65 us (2%)
    pallas_call x1, Pallas kernels, on_device(): pl.pallas_call(functools.partial(kernel, doms, modes), out_shape=pltpu.VM...  24.1 us
    pallas_call x1, Pallas kernels, on_device(): pl.pallas_call(finish_kernel, out_shape=(jax.ShapeDtypeStruct(stress.shap...  1.1 us

profile of v4, /device:TPU:387, one launch (start us, length us, event | category | flops | bytes accessed | tf_op | source)
XLA Modules:
  0.0 25.9 jit_solution(14451182955568230961)
XLA Ops:
  0.6 0.0 copy-start
  0.6 24.1 %ptt.1.pieces = bf16[18,80,256]{2,1,0:T(8,128)(2,1)S(1)} custom-call(bf16[3,17,4,256]{3,2,1,0:T(4,128)(2,1)} %bitcast.5, bf16[2,6,17,4,256]{4,3,2,1,0:T(4,128)(2,1)} %bitcast.4, f32[16]{0:T(128)} %relax.1, f32[16]{0:T(128)} %viscosity.1, f32[16]{0:T(128)} %extension.1, bf16[8,224,256]{2,1,0:T(8,128)(2,1)} %constant.10.clone.ahead_hbm, ...), custom_call_target="tpu_custom_call" | custom-call | tf_op jit(solution)/shard_map/ptt/pallas_call | solution.py:742
  24.8 0.0 copy-done
  24.8 1.1 %finish.1 = (bf16[2,6,17,4,256]{4,3,2,1,0:T(4,128)(2,1)}, f32[3,17,4,256]{3,2,1,0:T(4,128)}) custom-call(bf16[18,80,256]{2,1,0:T(8,128)(2,1)S(1)} %ptt.1.pieces, bf16[256,256]{1,0:T(8,128)(2,1)S(1)} %copy-done), custom_call_target="tpu_custom_call" | custom-call | tf_op jit(solution)/shard_map/finish/pallas_call | solution.py:763
Async XLA Ops:
  0.6 24.2 %copy-start = (bf16[256,256]{1,0:T(8,128)(2,1)S(1)}, bf16[256,256]{1,0:T(8,128)(2,1)}, u32[]{:S(2)}) copy-start(bf16[256,256]{1,0:T(8,128)(2,1)} %constant.14.clone.merge) | copy-start | bytes 393220
